TPU v7x, 256 devices: a whole 4x4x8 slice. The times are simulated.
256 devices in a mesh: src: 8 (over y, core), tgt: 32 (over x, z).
Axes of the slice: x: 4, y: 4, z: 8, core: 2. Of those that a mesh axis runs over, the one named last changes fastest.
Arguments:
- source: bfloat16 [16384, 128], P('src'), may hold values from -6 to 6
- target: bfloat16 [32768, 128], P('tgt'), may hold values from -5 to 5
- start_map: float32 [128, 128], replicated, may hold values from -1 to 1
- warm_potential: float32 [32768], P('tgt'), may hold values from -60 to 24
Outputs:
- row_potential: float32 [16384], P('src')
- col_potential: float32 [32768], P('tgt')
- new_map: float32 [128, 128], replicated
All inputs are finite; a program needn't handle non-finite values.
Results may differ from a plain program's by a relative error of at most 0.0078.
Values sent between devices are 32-bit elements; how exact they have to be, the bound alone decides.
A program may use at most 64 MiB of HBM per device.

v0:
```python
import math
import jax
import jax.numpy as jnp
from jax import lax
from jax.sharding import PartitionSpec as P

ROUNDS = 3
NEWTON = 10
EPS = 0.05


def row_partials(rotated, target, col_pot, score_scale):
    row_count = rotated.shape[0]
    block_rows = math.gcd(row_count, 512)
    blocks = rotated.reshape(row_count // block_rows, block_rows, rotated.shape[1])

    def row_one_block(row_block):
        scores = (
            jnp.einsum("rd,cd->rc", row_block, target, preferred_element_type=jnp.float32)
            * score_scale
            + col_pot[None, :]
        )
        peak_val = jnp.max(scores, axis=1)
        totals = jnp.sum(jnp.exp(scores - peak_val[:, None]), axis=1)
        return (peak_val, totals)

    peak_val, totals = lax.map(row_one_block, blocks)
    return (peak_val.reshape(row_count), totals.reshape(row_count))


def col_partials(rotated, target, row_pot, score_scale):
    row_count = rotated.shape[0]
    block_rows = math.gcd(row_count, 512)
    blocks = rotated.reshape(row_count // block_rows, block_rows, rotated.shape[1])
    pots = row_pot.reshape(row_count // block_rows, block_rows)

    def col_one_block(inputs):
        row_block, pot_block = inputs
        scores = (
            jnp.einsum("rd,cd->rc", row_block, target, preferred_element_type=jnp.float32)
            * score_scale
            + pot_block[:, None]
        )
        peak_val = jnp.max(scores, axis=0)
        totals = jnp.sum(jnp.exp(scores - peak_val[None, :]), axis=0)
        return (peak_val, totals)

    peaks, totals = lax.map(col_one_block, (blocks, pots))
    peak_val = jnp.max(peaks, axis=0)
    return (peak_val, jnp.sum(totals * jnp.exp(peaks - peak_val[None, :]), axis=0))


def across_targets(peak_val, totals):
    global_peak = lax.pmax(peak_val, "tgt")
    totals = lax.psum(totals * jnp.exp(peak_val - global_peak), "tgt")
    peak_val = global_peak
    return peak_val + jnp.log(totals)


def across_sources(peak_val, totals):
    global_peak = lax.pmax(peak_val, "src")
    totals = lax.psum(totals * jnp.exp(peak_val - global_peak), "src")
    peak_val = global_peak
    return peak_val + jnp.log(totals)


def polar(matrix):
    iterate = matrix / jnp.sqrt(jnp.sum(matrix * matrix) + 1e-06)
    for newton_index in range(NEWTON):
        gram_matrix = jnp.dot(iterate.T, iterate, precision=lax.Precision.HIGHEST)
        iterate = 1.5 * iterate - 0.5 * jnp.dot(
            iterate, gram_matrix, precision=lax.Precision.HIGHEST
        )
    return iterate


def shards(source, target, start_map, warm_potential):
    width = source.shape[1]
    score_scale = 1.0 / (math.sqrt(width) * EPS)
    rows_all = source.shape[0] * lax.axis_size("src")
    cols_all = target.shape[0] * lax.axis_size("tgt")
    rotated = jnp.dot(
        source, start_map.astype(jnp.bfloat16), preferred_element_type=jnp.float32
    ).astype(jnp.bfloat16)
    col_pot = warm_potential
    for round_index in range(ROUNDS):
        row_pot = -math.log(rows_all) - across_targets(
            *row_partials(rotated, target, col_pot, score_scale)
        )
        col_pot = -math.log(cols_all) - across_sources(
            *col_partials(rotated, target, row_pot, score_scale)
        )
    row_lse = across_targets(*row_partials(rotated, target, col_pot, score_scale))
    row_pot = -math.log(rows_all) - row_lse
    rows_here = source.shape[0] // lax.axis_size("tgt")
    block_rows = math.gcd(rows_here * lax.axis_size("tgt"), 512)
    nblocks = rows_here * lax.axis_size("tgt") // block_rows

    def numerator_one_block(inputs):
        row_block, lse_block = inputs
        scores = (
            jnp.einsum("rd,cd->rc", row_block, target, preferred_element_type=jnp.float32)
            * score_scale
            + col_pot[None, :]
            - lse_block[:, None]
        )
        weights = jnp.exp(scores).astype(jnp.bfloat16)
        return jnp.dot(weights, target, preferred_element_type=jnp.float32)

    parts_out = lax.map(
        numerator_one_block,
        (rotated.reshape(nblocks, block_rows, width), row_lse.reshape(nblocks, block_rows)),
    )
    my_targets = lax.psum_scatter(
        parts_out.reshape(rows_here * lax.axis_size("tgt"), width),
        "tgt",
        scatter_dimension=0,
        tiled=True,
    )
    source_rows = lax.dynamic_slice_in_dim(source, lax.axis_index("tgt") * rows_here, rows_here, 0)
    partial_value = jnp.einsum(
        "rd,re->de", source_rows.astype(jnp.float32), my_targets, precision=lax.Precision.HIGHEST
    )
    covariance_sum = lax.psum(partial_value, ("src", "tgt"))
    new_map = polar(covariance_sum)
    return (EPS * row_pot, EPS * col_pot, new_map)


def solution(mesh):
    placed = (P("src", None), P("tgt", None), P(), P("tgt"))
    return jax.shard_map(
        shards, mesh=mesh, in_specs=placed, out_specs=(P("src"), P("tgt"), P()), check_vma=False
    )
```

profile of v0, /device:TPU:1, one launch (start us, length us, event | category | flops | bytes accessed | tf_op | source)
XLA Modules:
  0.0 1202.2 jit_solution(3626454813866031106)
XLA Ops:
  9.4 8.7 while.94
  18.1 65.3 %pmax.49 = f32[2048]{0:T(1024)S(1)} all-reduce(f32[2048]{0:T(1024)S(1)} %bitcast.221), channel_id=1, replica_groups=mesh['src'=8,'tgt'=32] {'tgt'}, use_global_device_ids=true, to_apply=%region_4.5 | all-reduce | flops 2048 | bytes 16384 | tf_op jit(solution)/shard_map/pmax | solution.py:54
  83.4 56.8 %psum.56 = f32[2048]{0:T(1024)S(1)} all-reduce(f32[2048]{0:T(1024)S(1)} %exponential_multiply_fusion.3), channel_id=1, replica_groups=mesh['src'=8,'tgt'=32] {'tgt'}, use_global_device_ids=true, to_apply=%region_5.6 | all-reduce | flops 2048 | bytes 16384 | tf_op jit(solution)/shard_map/psum | solution.py:55
  140.3 8.4 while.95
  148.7 40.6 %pmax.50 = f32[1024]{0:T(1024)S(1)} all-reduce(f32[1024]{0:T(1024)S(1)} %reduce_max.90), channel_id=1, replica_groups=mesh['src'=8,'tgt'=32] {'src'}, use_global_device_ids=true, to_apply=%region_11.12 | all-reduce | flops 1024 | bytes 8192 | tf_op jit(solution)/shard_map/pmax | solution.py:61
  189.4 12.3 %psum.57 = f32[1024]{0:T(1024)S(1)} all-reduce(f32[1024]{0:T(1024)S(1)} %exponential_multiply_fusion.6), channel_id=1, replica_groups=mesh['src'=8,'tgt'=32] {'src'}, use_global_device_ids=true, to_apply=%region_13.14 | all-reduce | flops 1024 | bytes 8192 | tf_op jit(solution)/shard_map/psum | solution.py:62
  201.7 8.7 while.96
  210.4 58.5 %pmax.51 = f32[2048]{0:T(1024)S(1)} all-reduce(f32[2048]{0:T(1024)S(1)} %bitcast.223), channel_id=1, replica_groups=mesh['src'=8,'tgt'=32] {'tgt'}, use_global_device_ids=true, to_apply=%region_18.19 | all-reduce | flops 2048 | bytes 16384 | tf_op jit(solution)/shard_map/pmax | solution.py:54
  268.9 56.8 %psum.58 = f32[2048]{0:T(1024)S(1)} all-reduce(f32[2048]{0:T(1024)S(1)} %exponential_multiply_fusion.2), channel_id=1, replica_groups=mesh['src'=8,'tgt'=32] {'tgt'}, use_global_device_ids=true, to_apply=%region_19.20 | all-reduce | flops 2048 | bytes 16384 | tf_op jit(solution)/shard_map/psum | solution.py:55
  325.8 8.4 while.97
  334.2 40.5 %pmax.52 = f32[1024]{0:T(1024)S(1)} all-reduce(f32[1024]{0:T(1024)S(1)} %reduce_max.91), channel_id=1, replica_groups=mesh['src'=8,'tgt'=32] {'src'}, use_global_device_ids=true, to_apply=%region_25.26 | all-reduce | flops 1024 | bytes 8192 | tf_op jit(solution)/shard_map/pmax | solution.py:61
  374.8 12.4 %psum.59 = f32[1024]{0:T(1024)S(1)} all-reduce(f32[1024]{0:T(1024)S(1)} %exponential_multiply_fusion.5), channel_id=1, replica_groups=mesh['src'=8,'tgt'=32] {'src'}, use_global_device_ids=true, to_apply=%region_27.28 | all-reduce | flops 1024 | bytes 8192 | tf_op jit(solution)/shard_map/psum | solution.py:62
  387.2 8.7 while.98
  395.9 59.2 %pmax.53 = f32[2048]{0:T(1024)S(1)} all-reduce(f32[2048]{0:T(1024)S(1)} %bitcast.225), channel_id=1, replica_groups=mesh['src'=8,'tgt'=32] {'tgt'}, use_global_device_ids=true, to_apply=%region_32.33 | all-reduce | flops 2048 | bytes 16384 | tf_op jit(solution)/shard_map/pmax | solution.py:54
  455.1 57.0 %psum.60 = f32[2048]{0:T(1024)S(1)} all-reduce(f32[2048]{0:T(1024)S(1)} %exponential_multiply_fusion.1), channel_id=1, replica_groups=mesh['src'=8,'tgt'=32] {'tgt'}, use_global_device_ids=true, to_apply=%region_33.34 | all-reduce | flops 2048 | bytes 16384 | tf_op jit(solution)/shard_map/psum | solution.py:55
  512.2 8.4 while.99
  520.6 39.6 %pmax.54 = f32[1024]{0:T(1024)S(1)} all-reduce(f32[1024]{0:T(1024)S(1)} %reduce_max.92), channel_id=1, replica_groups=mesh['src'=8,'tgt'=32] {'src'}, use_global_device_ids=true, to_apply=%region_39.40 | all-reduce | flops 1024 | bytes 8192 | tf_op jit(solution)/shard_map/pmax | solution.py:61
  560.3 12.4 %psum.61 = f32[1024]{0:T(1024)S(1)} all-reduce(f32[1024]{0:T(1024)S(1)} %exponential_multiply_fusion.4), channel_id=1, replica_groups=mesh['src'=8,'tgt'=32] {'src'}, use_global_device_ids=true, to_apply=%region_41.42 | all-reduce | flops 1024 | bytes 8192 | tf_op jit(solution)/shard_map/psum | solution.py:62
  573.3 8.7 while.100
  582.1 59.2 %pmax.55 = f32[2048]{0:T(1024)S(1)} all-reduce(f32[2048]{0:T(1024)S(1)} %bitcast.227), channel_id=1, replica_groups=mesh['src'=8,'tgt'=32] {'tgt'}, use_global_device_ids=true, to_apply=%region_46.47 | all-reduce | flops 2048 | bytes 16384 | tf_op jit(solution)/shard_map/pmax | solution.py:54
  641.3 57.0 %psum.62 = f32[2048]{0:T(1024)S(1)} all-reduce(f32[2048]{0:T(1024)S(1)} %exponential_multiply_fusion), channel_id=1, replica_groups=mesh['src'=8,'tgt'=32] {'tgt'}, use_global_device_ids=true, to_apply=%region_47.48 | all-reduce | flops 2048 | bytes 16384 | tf_op jit(solution)/shard_map/psum | solution.py:55
  698.9 10.4 while.101
  709.6 228.3 %reduce-scatter.2.cloned.1.call-done = f32[64,128]{1,0:T(8,128)} async-done(((f32[2048,128]{1,0:T(8,128)}), f32[64,128]{1,0:T(8,128)}) %reduce-scatter.2.cloned.1.call-update) | async-done | bytes 32784 | tf_op jit(solution)/shard_map/reduce_scatter | solution.py:114
  939.5 246.2 %all-reduce.2.cloned.1.call-done = f32[128,128]{1,0:T(8,128)} async-done(((f32[128,128]{1,0:T(8,128)}), f32[128,128]{1,0:T(8,128)}) %all-reduce.2.cloned.1.call-update) | async-done | bytes 65552 | tf_op jit(solution)/shard_map/psum | solution.py:124
  (216 shorter events, 83.7 us)
Async XLA Ops:
  7.2 1.0 copy-start
  7.2 930.7 %reduce-scatter.2.cloned.1.call-start = ((), (), s32[]{:S(2)}) async-start(), calls=%async_computation.1 | async-start | bytes 1081344 | tf_op jit(solution)/shard_map/reduce_scatter | solution.py:114
  9.4 1.5 copy-start.1
  11.6 1.5 copy-start.1
  13.7 1.5 copy-start.1
  15.9 1.5 copy-start.1
  709.4 476.4 %all-reduce.2.cloned.1.call-start = ((), (), s32[]{:S(2)}) async-start(), calls=%async_computation.2 | async-start | bytes 131072 | tf_op jit(solution)/shard_map/psum | solution.py:124
Sparse Core Ops, SparseCore 0:
  709.5 228.3 reduce-scatter.1
  944.0 241.7 all-reduce.1
where the time goes:
time: 1200 us
  blocking collectives  628 us (52%)
  waiting for transfers between devices  475 us (40%)
  matrix products  60.8 us (5%)
  other arithmetic  18 us (2%)
  between operations  15.3 us (1%)
    psum x1, waiting for transfers between devices, shards(): covariance_sum = lax.psum(partial_value, ('src', 'tgt'))  246 us
    pmax x4, blocking collectives, across_targets(): global_peak = lax.pmax(peak_val, 'tgt')  242 us
    reduce_scatter x1, waiting for transfers between devices, shards(): lax.psum_scatter(parts_out.reshape(rows_here * lax.axis_size('tgt'), widt...  228 us
    psum x4, blocking collectives, across_targets(): totals = lax.psum(totals * jnp.exp(peak_val - global_peak), 'tgt')  228 us
    pmax x3, blocking collectives, across_sources(): global_peak = lax.pmax(peak_val, 'src')  121 us
    psum x3, blocking collectives, across_sources(): totals = lax.psum(totals * jnp.exp(peak_val - global_peak), 'src')  37.1 us
  transfers between devices with their start and end apart: 2, of which 2 were waited for; matrix products, arithmetic and copies ran while one was open for 0% of the time, Pallas kernels for 0%

commit v1 on v0

--- a/solution.py
+++ b/solution.py
@@ -121,7 +121,7 @@
     partial_value = jnp.einsum(
         "rd,re->de", source_rows.astype(jnp.float32), my_targets, precision=lax.Precision.HIGHEST
     )
-    covariance_sum = lax.psum(partial_value, ("src", "tgt"))
+    covariance_sum = lax.psum(lax.psum(partial_value, "tgt"), "src")
     new_map = polar(covariance_sum)
     return (EPS * row_pot, EPS * col_pot, new_map)
 

time: 1200 us -> 1170 us (0.975)
  waiting for transfers between devices: 475 us -> 436 us
    psum x1 -> x2, waiting for transfers between devices: 246 us -> 207 us  [shards(): covariance_sum = lax.psum(lax.psum(partial_value, 'tgt'), 'src')]
  transfers between devices with their start and end apart: 2 -> 3, of which waited for: 2 -> 3; matrix products, arithmetic and copies ran while one was open for 0% -> 0% of each run, Pallas kernels for 0% -> 0%
where the time goes in v1:
time: 1170 us; the launch traced here: 1160 us
  blocking collectives  628 us (54%)
  waiting for transfers between devices  436 us (37%)
  matrix products  60.8 us (5%)
  other arithmetic  18 us (2%)
  between operations  15 us (1%)
    pmax x4, blocking collectives, across_targets(): global_peak = lax.pmax(peak_val, 'tgt')  242 us
    reduce_scatter x1, waiting for transfers between devices, shards(): lax.psum_scatter(parts_out.reshape(rows_here * lax.axis_size('tgt'), widt...  228 us
    psum x4, blocking collectives, across_targets(): totals = lax.psum(totals * jnp.exp(peak_val - global_peak), 'tgt')  228 us
    psum x2, waiting for transfers between devices, shards(): covariance_sum = lax.psum(lax.psum(partial_value, 'tgt'), 'src')  207 us
    pmax x3, blocking collectives, across_sources(): global_peak = lax.pmax(peak_val, 'src')  121 us
    psum x3, blocking collectives, across_sources(): totals = lax.psum(totals * jnp.exp(peak_val - global_peak), 'src')  37.1 us
    dot_general x16, matrix products, row_one_block(): jnp.einsum('rd,cd->rc', row_block, target, preferred_element_type=jnp.flo...  23.5 us
  transfers between devices with their start and end apart: 3, of which 3 were waited for; matrix products, arithmetic and copies ran while one was open for 0% of the time, Pallas kernels for 0%

profile of v1, /device:TPU:1, one launch (start us, length us, event | category | flops | bytes accessed | tf_op | source)
XLA Modules:
  0.0 1163.4 jit_solution(8729864090589498516)
XLA Ops:
  9.4 8.7 while.94
  18.1 65.3 %pmax.49 = f32[2048]{0:T(1024)S(1)} all-reduce(f32[2048]{0:T(1024)S(1)} %bitcast.221), channel_id=1, replica_groups=mesh['src'=8,'tgt'=32] {'tgt'}, use_global_device_ids=true, to_apply=%region_4.5 | all-reduce | flops 2048 | bytes 16384 | tf_op jit(solution)/shard_map/pmax | solution.py:54
  83.4 56.8 %psum.63 = f32[2048]{0:T(1024)S(1)} all-reduce(f32[2048]{0:T(1024)S(1)} %exponential_multiply_fusion.3), channel_id=1, replica_groups=mesh['src'=8,'tgt'=32] {'tgt'}, use_global_device_ids=true, to_apply=%region_5.6 | all-reduce | flops 2048 | bytes 16384 | tf_op jit(solution)/shard_map/psum | solution.py:55
  140.3 8.4 while.95
  148.7 40.6 %pmax.50 = f32[1024]{0:T(1024)S(1)} all-reduce(f32[1024]{0:T(1024)S(1)} %reduce_max.90), channel_id=1, replica_groups=mesh['src'=8,'tgt'=32] {'src'}, use_global_device_ids=true, to_apply=%region_11.12 | all-reduce | flops 1024 | bytes 8192 | tf_op jit(solution)/shard_map/pmax | solution.py:61
  189.4 12.3 %psum.64 = f32[1024]{0:T(1024)S(1)} all-reduce(f32[1024]{0:T(1024)S(1)} %exponential_multiply_fusion.6), channel_id=1, replica_groups=mesh['src'=8,'tgt'=32] {'src'}, use_global_device_ids=true, to_apply=%region_13.14 | all-reduce | flops 1024 | bytes 8192 | tf_op jit(solution)/shard_map/psum | solution.py:62
  201.7 8.7 while.96
  210.4 58.5 %pmax.51 = f32[2048]{0:T(1024)S(1)} all-reduce(f32[2048]{0:T(1024)S(1)} %bitcast.223), channel_id=1, replica_groups=mesh['src'=8,'tgt'=32] {'tgt'}, use_global_device_ids=true, to_apply=%region_18.19 | all-reduce | flops 2048 | bytes 16384 | tf_op jit(solution)/shard_map/pmax | solution.py:54
  268.9 56.8 %psum.65 = f32[2048]{0:T(1024)S(1)} all-reduce(f32[2048]{0:T(1024)S(1)} %exponential_multiply_fusion.2), channel_id=1, replica_groups=mesh['src'=8,'tgt'=32] {'tgt'}, use_global_device_ids=true, to_apply=%region_19.20 | all-reduce | flops 2048 | bytes 16384 | tf_op jit(solution)/shard_map/psum | solution.py:55
  325.8 8.4 while.97
  334.2 40.5 %pmax.52 = f32[1024]{0:T(1024)S(1)} all-reduce(f32[1024]{0:T(1024)S(1)} %reduce_max.91), channel_id=1, replica_groups=mesh['src'=8,'tgt'=32] {'src'}, use_global_device_ids=true, to_apply=%region_25.26 | all-reduce | flops 1024 | bytes 8192 | tf_op jit(solution)/shard_map/pmax | solution.py:61
  374.8 12.4 %psum.66 = f32[1024]{0:T(1024)S(1)} all-reduce(f32[1024]{0:T(1024)S(1)} %exponential_multiply_fusion.5), channel_id=1, replica_groups=mesh['src'=8,'tgt'=32] {'src'}, use_global_device_ids=true, to_apply=%region_27.28 | all-reduce | flops 1024 | bytes 8192 | tf_op jit(solution)/shard_map/psum | solution.py:62
  387.2 8.7 while.98
  395.9 59.2 %pmax.53 = f32[2048]{0:T(1024)S(1)} all-reduce(f32[2048]{0:T(1024)S(1)} %bitcast.225), channel_id=1, replica_groups=mesh['src'=8,'tgt'=32] {'tgt'}, use_global_device_ids=true, to_apply=%region_32.33 | all-reduce | flops 2048 | bytes 16384 | tf_op jit(solution)/shard_map/pmax | solution.py:54
  455.1 57.0 %psum.67 = f32[2048]{0:T(1024)S(1)} all-reduce(f32[2048]{0:T(1024)S(1)} %exponential_multiply_fusion.1), channel_id=1, replica_groups=mesh['src'=8,'tgt'=32] {'tgt'}, use_global_device_ids=true, to_apply=%region_33.34 | all-reduce | flops 2048 | bytes 16384 | tf_op jit(solution)/shard_map/psum | solution.py:55
  520.6 39.6 %pmax.54 = f32[1024]{0:T(1024)S(1)} all-reduce(f32[1024]{0:T(1024)S(1)} %reduce_max.92), channel_id=1, replica_groups=mesh['src'=8,'tgt'=32] {'src'}, use_global_device_ids=true, to_apply=%region_39.40 | all-reduce | flops 1024 | bytes 8192 | tf_op jit(solution)/shard_map/pmax | solution.py:61
  560.3 12.4 %psum.68 = f32[1024]{0:T(1024)S(1)} all-reduce(f32[1024]{0:T(1024)S(1)} %exponential_multiply_fusion.4), channel_id=1, replica_groups=mesh['src'=8,'tgt'=32] {'src'}, use_global_device_ids=true, to_apply=%region_41.42 | all-reduce | flops 1024 | bytes 8192 | tf_op jit(solution)/shard_map/psum | solution.py:62
  573.3 8.7 while.100
  582.1 59.2 %pmax.55 = f32[2048]{0:T(1024)S(1)} all-reduce(f32[2048]{0:T(1024)S(1)} %bitcast.227), channel_id=1, replica_groups=mesh['src'=8,'tgt'=32] {'tgt'}, use_global_device_ids=true, to_apply=%region_46.47 | all-reduce | flops 2048 | bytes 16384 | tf_op jit(solution)/shard_map/pmax | solution.py:54
  641.3 57.0 %psum.69 = f32[2048]{0:T(1024)S(1)} all-reduce(f32[2048]{0:T(1024)S(1)} %exponential_multiply_fusion), channel_id=1, replica_groups=mesh['src'=8,'tgt'=32] {'tgt'}, use_global_device_ids=true, to_apply=%region_47.48 | all-reduce | flops 2048 | bytes 16384 | tf_op jit(solution)/shard_map/psum | solution.py:55
  698.9 10.4 while.101
  709.4 228.5 %reduce-scatter.2.cloned.1.call-done = f32[64,128]{1,0:T(8,128)} async-done(((f32[2048,128]{1,0:T(8,128)}), f32[64,128]{1,0:T(8,128)}) %reduce-scatter.2.cloned.1.call-update) | async-done | bytes 32784 | tf_op jit(solution)/shard_map/reduce_scatter | solution.py:114
  939.8 140.9 %all-reduce.3.cloned.1.call-done = f32[128,128]{1,0:T(8,128)} async-done(((f32[128,128]{1,0:T(8,128)}), f32[128,128]{1,0:T(8,128)}) %all-reduce.3.cloned.1.call-update) | async-done | bytes 65552 | tf_op jit(solution)/shard_map/psum | solution.py:124
  1080.7 66.4 %all-reduce.5.cloned.1.call-done = f32[128,128]{1,0:T(8,128)} async-done(((f32[128,128]{1,0:T(8,128)}), f32[128,128]{1,0:T(8,128)}) %all-reduce.5.cloned.1.call-update) | async-done | bytes 65552 | tf_op jit(solution)/shard_map/psum | solution.py:124
  (219 shorter events, 92.1 us)
Async XLA Ops:
  7.2 1.0 copy-start
  7.2 930.7 %reduce-scatter.2.cloned.1.call-start = ((), (), s32[]{:S(2)}) async-start(), calls=%async_computation.1 | async-start | bytes 1081344 | tf_op jit(solution)/shard_map/reduce_scatter | solution.py:114
  9.4 1.5 copy-start.1
  11.6 1.5 copy-start.1
  13.7 1.5 copy-start.1
  15.9 1.5 copy-start.1
  709.4 371.3 %all-reduce.3.cloned.1.call-start = ((), (), s32[]{:S(2)}) async-start(), calls=%async_computation.2 | async-start | bytes 131072 | tf_op jit(solution)/shard_map/psum | solution.py:124
  939.5 207.6 %all-reduce.5.cloned.1.call-start = ((), (), s32[]{:S(2)}) async-start(), calls=%async_computation.3 | async-start | bytes 131072 | tf_op jit(solution)/shard_map/psum | solution.py:124
Sparse Core Ops, SparseCore 0:
  709.5 228.3 reduce-scatter.1
  941.9 138.7 all-reduce.2
  1083.0 64.0 all-reduce.4
